TPU v7x, 32 devices: a whole 2x2x4 slice. The times are simulated.
32 devices in a mesh: llm: 4 (over y, x), enc: 8 (over z, core).
Axes of the slice: x: 2, y: 2, z: 4, core: 2. Of those that a mesh axis runs over, the one named last changes fastest.
Arguments:
- token_gradient: bfloat16 [64, 128, 8192], P('enc', None, 'llm'), may hold values from -6 to 6
- projection: bfloat16 [1280, 8192], P(None, 'llm'), may hold values from -0.0625 to 0.0625
- clip_length: int32 [128], P('enc'), may hold values from 16 to 32, as said below
- clip_offset: int32 [128], P('enc'), may hold values from 0 to 96, as said below
- clip_home: int32 [128], P('enc'), may hold values from 0 to 127, as said below
- block_input: bfloat16 [128, 32, 1280], P('enc'), may hold values from -6 to 6
- block_output: bfloat16 [128, 32, 1280], P('enc'), may hold values from -6 to 6
- norm_gain: float32 [1280], replicated, may hold values from 0.1 to 1.9
- norm_bias: float32 [1280], replicated, may hold values from -3 to 3
- up_weight: bfloat16 [1280, 5120], P('enc', 'llm'), may hold values from -0.15625 to 0.15625
- up_bias: float32 [5120], P('llm'), may hold values from -3 to 3
- down_weight: bfloat16 [5120, 1280], P('llm', 'enc'), may hold values from -0.078125 to 0.078125
- post_gain: float32 [1280], replicated, may hold values from 0.1 to 1.9
Outputs:
- input_gradient: bfloat16 [128, 32, 1280], P('enc', None, 'llm')
- up_gradient: float32 [1280, 5120], P('enc', 'llm')
- down_gradient: float32 [5120, 1280], P('llm', 'enc')
Inputs may be any that keep to these rules, and one draw needn't show every extreme that they name: `clip_length`: each entry of an aligned block of 16 entries is at most 32, and every block holds one entry equal to 32. Clip k starts in part k % 2 of its sequence, the parts being 64 rows long, and clip_offset + 32 stays within that part. `clip_home`: A permutation of the 128 encoder slots; slot j belongs to encoder index j // 16; the clips of one aligned block of 16 entries go to one encoder index at most 2 times, and some encoder index receives exactly 2 of them.
All inputs are finite; a program needn't handle non-finite values.
Results may differ from a plain program's by a relative error of at most 0.0068.
Values may be sent and summed in bfloat16 or wider, within the bound.
A program may use at most 128 MiB of HBM per device.

v0:
```python
import jax
import jax.numpy as jnp
from jax import lax
from jax.sharding import PartitionSpec as P

CPS = 2


norm_epsilon = 1e-05


def gelu_parts(pre_act):
    normal_cdf = 0.5 * (1.0 + jax.scipy.special.erf(pre_act * 0.7071067811865476))
    normal_pdf = jnp.exp(-0.5 * pre_act * pre_act) * 0.3989422804014327
    return (pre_act * normal_cdf, normal_cdf + pre_act * normal_pdf)


def norm_stats(values):
    row_mean = jnp.mean(values, axis=-1, keepdims=True)
    centred = values - row_mean
    variance = jnp.mean(centred * centred, axis=-1, keepdims=True)
    inverse = lax.rsqrt(variance + norm_epsilon)
    return (centred * inverse, inverse)


def norm_backward(grad_hat, normed_hat, inverse):
    first_mean = jnp.mean(grad_hat, axis=-1, keepdims=True)
    second_mean = jnp.mean(grad_hat * normed_hat, axis=-1, keepdims=True)
    return inverse * (grad_hat - first_mean - normed_hat * second_mean)


def row_contract(left_rows, right_rows):
    return lax.dot_general(
        left_rows, right_rows, (((0,), (0,)), ((), ())), preferred_element_type=jnp.float32
    )


def own_columns(values, column_start, column_span):
    return lax.dynamic_slice_in_dim(values, column_start, column_span, values.ndim - 1)


def project_terms(clip_blocks, projection):
    clips_here, frames, columns = clip_blocks.shape
    flat_rows = clip_blocks.reshape(clips_here * frames, columns)
    partial_terms = lax.dot_general(
        flat_rows, projection, (((1,), (1,)), ((), ())), preferred_element_type=jnp.float32
    )
    return partial_terms.reshape(clips_here, frames, projection.shape[0])


def project_sum(clip_blocks, projection):
    return lax.psum(project_terms(clip_blocks, projection), "llm")


def deliver(clip_blocks, routing, slot_marks):
    clips_here, frames, columns = clip_blocks.shape
    devices, pair_slots, slot_count = slot_marks.shape
    packed = jnp.einsum(
        "bc,cfw->bfw", routing, clip_blocks, preferred_element_type=jnp.float32
    ).astype(jnp.bfloat16)
    packed = packed.reshape(devices, pair_slots, frames, columns)
    received, marks_in = (
        lax.all_to_all(packed, "enc", split_axis=0, concat_axis=0, tiled=True),
        lax.all_to_all(slot_marks, "enc", split_axis=0, concat_axis=0, tiled=True),
    )
    placed = jnp.einsum("npc,npfw->cfw", marks_in, received, preferred_element_type=jnp.float32)
    return placed.astype(jnp.bfloat16)


def shards(
    token_gradient,
    projection,
    clip_length,
    clip_offset,
    clip_home,
    block_input,
    block_output,
    norm_gain,
    norm_bias,
    up_weight,
    up_bias,
    down_weight,
    post_gain,
):
    devices = lax.axis_size("enc")
    clips_here, frames, model_width = block_input.shape
    pair_slots = max(1, clips_here // devices)
    positions = jnp.arange(frames, dtype=jnp.int32)
    clip_order = jnp.arange(clips_here, dtype=jnp.int32)
    target = clip_home // clips_here
    slot_place = clip_home % clips_here
    earlier = clip_order[None, :] < clip_order[:, None]
    same_target = target[None, :] == target[:, None]
    bucket_rank = jnp.sum((earlier & same_target).astype(jnp.int32), axis=1)
    bucket = target * pair_slots + bucket_rank
    buckets = jnp.arange(devices * pair_slots, dtype=jnp.int32)
    routing = (buckets[:, None] == bucket[None, :]).astype(jnp.bfloat16)
    slot_table = (slot_place[:, None] == clip_order[None, :]).astype(jnp.bfloat16)
    slot_marks = jnp.dot(routing, slot_table, preferred_element_type=jnp.float32).astype(
        jnp.bfloat16
    )
    slot_marks = slot_marks.reshape(devices, pair_slots, clips_here)

    def cut_clip(clip_index, offset, length):
        picked = lax.dynamic_slice(
            token_gradient,
            (clip_index // CPS, offset, jnp.int32(0)),
            (1, frames, token_gradient.shape[2]),
        )[0]
        return jnp.where((positions < length)[:, None], picked, jnp.zeros_like(picked))

    clip_blocks = jax.vmap(cut_clip)(clip_order, clip_offset, clip_length)
    feature_grad = project_sum(deliver(clip_blocks, routing, slot_marks), projection).astype(
        jnp.bfloat16
    )
    row_total = clips_here * frames
    feature_rows = feature_grad.reshape(row_total, model_width).astype(jnp.float32)
    output_hat, output_inverse = norm_stats(
        block_output.reshape(row_total, model_width).astype(jnp.float32)
    )
    post_grad = norm_backward(feature_rows * post_gain, output_hat, output_inverse)
    post_rounded = post_grad.astype(jnp.bfloat16)
    input_hat, input_inverse = norm_stats(
        block_input.reshape(row_total, model_width).astype(jnp.float32)
    )
    normed = (input_hat * norm_gain + norm_bias).astype(jnp.bfloat16)
    up_full, down_full = (
        lax.all_gather(up_weight, "enc", axis=0, tiled=True),
        lax.all_gather(down_weight, "enc", axis=1, tiled=True),
    )
    pre_act = jnp.dot(normed, up_full, preferred_element_type=jnp.float32) + up_bias
    activation, gelu_slope = gelu_parts(pre_act)
    act_rounded = activation.astype(jnp.bfloat16)
    act_grad = lax.dot_general(
        post_rounded, down_full, (((1,), (1,)), ((), ())), preferred_element_type=jnp.float32
    )
    pre_grad = (act_grad * gelu_slope).astype(jnp.bfloat16)
    normed_part = lax.dot_general(
        pre_grad, up_full, (((1,), (1,)), ((), ())), preferred_element_type=jnp.float32
    )
    groups = lax.axis_size("llm")
    share_width = model_width // groups
    share_start = lax.axis_index("llm") * share_width
    normed_grad = lax.psum(normed_part, "llm")
    full_grad = post_grad + norm_backward(normed_grad * norm_gain, input_hat, input_inverse)
    input_rows = own_columns(full_grad, share_start, share_width)
    input_gradient = input_rows.astype(jnp.bfloat16).reshape(clips_here, frames, share_width)
    scale_count = clips_here * devices
    up_gradient = (
        lax.psum_scatter(
            row_contract(
                own_columns(normed, jnp.int32(0), up_weight.shape[0] * lax.axis_size("enc")),
                pre_grad,
            ),
            "enc",
            scatter_dimension=0,
            tiled=True,
        )
        / scale_count
    )
    down_gradient = (
        lax.psum_scatter(
            row_contract(
                own_columns(
                    post_rounded, jnp.int32(0), down_weight.shape[1] * lax.axis_size("enc")
                ),
                act_rounded,
            ),
            "enc",
            scatter_dimension=0,
            tiled=True,
        )
        / scale_count
    ).T
    return (input_gradient, up_gradient, down_gradient)


def solution(mesh):
    return jax.shard_map(
        shards,
        mesh=mesh,
        in_specs=(
            P("enc", None, "llm"),
            P(None, "llm"),
            P("enc"),
            P("enc"),
            P("enc"),
            P("enc", None, None),
            P("enc", None, None),
            P(),
            P(),
            P("enc", "llm"),
            P("llm"),
            P("llm", "enc"),
            P(),
        ),
        out_specs=(P("enc", None, "llm"), P("enc", "llm"), P("llm", "enc")),
        check_vma=False,
    )
```

profile of v0, /device:TPU:0, one launch (start us, length us, event | category | flops | bytes accessed | tf_op | source)
XLA Modules:
  0.0 480.9 jit_solution(16181724858941878822)
XLA Ops:
  9.5 6.3 %all-to-all-start = ((bf16[8,2,16]{2,1,0:T(2,128)(2,1)}), bf16[8,2,16]{2,1,0:T(2,128)(2,1)S(1)}, u32[]{:S(2)}, u32[]{:S(2)}) async-start(bf16[8,2,16]{2,1,0:T(2,128)(2,1)} %bitcast), calls=%async_computation | async-start | bytes 8192 | tf_op jit(solution)/shard_map/all_to_all | solution.py:64
  15.9 6.4 %copy.24 = bf16[8,128,2048]{2,0,1:T(8,128)(2,1)} copy(bf16[8,128,2048]{2,1,0:T(8,128)(2,1)} %param.13) | data formatting | bytes 8388608 | tf_op args[0]
  22.3 5.8 %gather_fusion = bf16[16,32,2048]{2,0,1:T(8,128)(2,1)S(1)} fusion(bf16[8,128,2048]{2,0,1:T(8,128)(2,1)} %copy.24, s32[16]{0:T(128)S(1)} %fusion.36), kind=kCustom, calls=%fused_computation | custom fusion | bytes 4194496 | tf_op jit(solution)/shard_map/vmap()/gather | solution.py:105
  28.1 2.1 convolution_convert_fusion
  30.3 3.2 reshape.211
  33.4 3.1 copy.25
  36.5 5.4 %all-to-all-start.1 = ((bf16[8,2,32,2048]{3,1,2,0:T(2,128)(2,1)}), bf16[8,2,32,2048]{3,1,2,0:T(2,128)(2,1)}, u32[]{:S(2)}, u32[]{:S(2)}) async-start(bf16[8,2,32,2048]{3,1,2,0:T(2,128)(2,1)} %copy.25), calls=%async_computation.1 | async-start | bytes 4194304 | tf_op jit(solution)/shard_map/all_to_all | solution.py:63
  46.6 72.3 %all-to-all-done.1 = bf16[8,2,32,2048]{3,1,2,0:T(2,128)(2,1)} async-done(((bf16[8,2,32,2048]{3,1,2,0:T(2,128)(2,1)}), bf16[8,2,32,2048]{3,1,2,0:T(2,128)(2,1)}, u32[]{:S(2)}, u32[]{:S(2)}) %all-to-all-start.1) | async-done | bytes 2097184 | tf_op jit(solution)/shard_map/all_to_all | solution.py:63
  118.9 2.9 bitcast_convert_fusion
  121.8 8.2 %fusion = f32[16,32,1280]{2,1,0:T(8,128)} fusion(bf16[1280,2048]{1,0:T(8,128)(2,1)} %param.14, bf16[16,32,2048]{2,0,1:T(8,128)(2,1)S(1)} %bitcast_convert_fusion), kind=kOutput, calls=%fused_computation.1 | convolution fusion | flops 2684354560 | bytes 9961472 | tf_op jit(solution)/shard_map/dot_general | solution.py:45
  130.1 93.4 %all-reduce.4 = bf16[16,32,1280]{2,1,0:T(8,128)(2,1)} all-reduce(f32[16,32,1280]{2,1,0:T(8,128)} %fusion), channel_id=1, replica_groups=mesh['llm'=4,'enc'=8] {'llm'}, use_global_device_ids=true, to_apply=%region_3.4 | all-reduce | flops 655360 | bytes 3932160 | tf_op jit(solution)/shard_map/psum | solution.py:52
  223.4 2.1 multiply_reduce_fusion.4
  225.7 3.7 fusion.11
  229.4 6.0 %convolution_add_fusion = f32[512,1280]{1,0:T(8,128)} fusion(bf16[1280,1280]{1,0:T(8,128)(2,1)} %all-gather.5.cloned.1.call-done, f32[1280]{0:T(1024)S(1)} %copy-done.6, f32[512,1280]{1,0:T(8,128)} %fusion.7, f32[1280]{0:T(1024)S(1)} %copy-done.7, f32[1280]{0:T(1024)S(1)} %copy-done.3), kind=kOutput, calls=%fused_computation.6 | convolution fusion | flops 1680343040 | bytes 8535040 | tf_op jit(solution)/shard_map/dot_general | solution.py:131
  235.5 5.9 %fusion.2 = bf16[512,1280]{1,0:T(8,128)(2,1)S(1)} fusion(bf16[1280,1280]{0,1:T(8,128)(2,1)} %all-gather.3.cloned.1.call-done, f32[512,1280]{1,0:T(8,128)} %convolution_add_fusion, f32[512,1280]{1,0:T(8,128)} %fusion.11), kind=kOutput, calls=%fused_computation.8 | convolution fusion | flops 1684930560 | bytes 9830400 | tf_op jit(solution)/shard_map/dot_general | solution.py:134
  241.4 3.4 fusion.42
  244.9 6.4 %fusion.24 = f32[1280,1280]{1,0:T(8,128)} fusion(bf16[512,1280]{1,0:T(8,128)(2,1)S(1)} %fusion.2, f32[512,1280]{1,0:T(8,128)} %fusion.7, f32[1280]{0:T(1024)S(1)} %copy-done.7, f32[1280]{0:T(1024)S(1)} %copy-done.3), kind=kOutput, calls=%fused_computation.50 | convolution fusion | flops 1679687680 | bytes 10496000 | tf_op jit(solution)/shard_map/dot_general | solution.py:33
  251.6 7.4 %fusion.17 = f32[1280,1280]{1,0:T(8,128)} fusion(f32[512,1280]{1,0:T(8,128)} %convolution_add_fusion, f32[512,1280]{1,0:T(8,128)} %fusion.11), kind=kOutput, calls=%fused_computation.35 | convolution fusion | flops 1681653760 | bytes 11796480 | tf_op jit(solution)/shard_map/dot_general | solution.py:33
  259.0 65.7 %all-reduce.3.cloned.1.call-done = f32[512,1280]{1,0:T(8,128)} async-done(((f32[512,1280]{1,0:T(8,128)}), f32[512,1280]{1,0:T(8,128)}) %all-reduce.3.cloned.1.call-update) | async-done | bytes 2621456 | tf_op jit(solution)/shard_map/psum | solution.py:144
  324.8 2.6 fusion.41
  327.4 3.3 fusion.19
  330.7 68.7 %reduce-scatter.3.cloned.1.call-done = f32[160,1280]{1,0:T(8,128)} async-done(((f32[1280,1280]{1,0:T(8,128)}), f32[160,1280]{1,0:T(8,128)}) %reduce-scatter.3.cloned.1.call-update) | async-done | bytes 819216 | tf_op jit(solution)/shard_map/reduce_scatter | solution.py:150
  399.4 2.1 broadcast_multiply_fusion.1
  401.4 70.9 %reduce-scatter.5.cloned.1.call-done = f32[160,1280]{1,0:T(8,128)} async-done(((f32[1280,1280]{1,0:T(8,128)}), f32[160,1280]{1,0:T(8,128)}) %reduce-scatter.5.cloned.1.call-update) | async-done | bytes 819216 | tf_op jit(solution)/shard_map/reduce_scatter | solution.py:162
  (56 shorter events, 9.6 us)
Async XLA Ops:
  7.2 222.2 %all-gather.5.cloned.1.call-start = ((), (), s32[]{:S(2)}) async-start(), calls=%async_computation.5 | async-start | bytes 3686400 | tf_op jit(solution)/shard_map/all_gather | solution.py:128
  9.5 27.0 %all-to-all-start = ((bf16[8,2,16]{2,1,0:T(2,128)(2,1)}), bf16[8,2,16]{2,1,0:T(2,128)(2,1)S(1)}, u32[]{:S(2)}, u32[]{:S(2)}) async-start(bf16[8,2,16]{2,1,0:T(2,128)(2,1)} %bitcast), calls=%async_computation | async-start | bytes 8192 | tf_op jit(solution)/shard_map/all_to_all | solution.py:64
  15.9 6.4 %copy-start.8 = (s32[16]{0:T(128)S(1)}, s32[16]{0:T(128)}, u32[]{:S(2)}) copy-start(s32[16]{0:T(128)} %param.16) | copy-start | bytes 196
  22.3 5.8 %copy-start.4 = (s32[16]{0:T(128)S(1)}, s32[16]{0:T(128)}, u32[]{:S(2)}) copy-start(s32[16]{0:T(128)} %param.15) | copy-start | bytes 196
  36.5 6.4 %copy-start = (bf16[16,32,1280]{2,1,0:T(8,128)(2,1)S(1)}, bf16[16,32,1280]{2,1,0:T(8,128)(2,1)}, u32[]{:S(2)}) copy-start(bf16[16,32,1280]{2,1,0:T(8,128)(2,1)} %param.19) | copy-start | bytes 3932164
  36.5 7.3 %copy-start.1 = (bf16[16,32,1280]{2,1,0:T(8,128)(2,1)S(1)}, bf16[16,32,1280]{2,1,0:T(8,128)(2,1)}, u32[]{:S(2)}) copy-start(bf16[16,32,1280]{2,1,0:T(8,128)(2,1)} %param.18) | copy-start | bytes 3932164
  36.5 82.3 %all-to-all-start.1 = ((bf16[8,2,32,2048]{3,1,2,0:T(2,128)(2,1)}), bf16[8,2,32,2048]{3,1,2,0:T(2,128)(2,1)}, u32[]{:S(2)}, u32[]{:S(2)}) async-start(bf16[8,2,32,2048]{3,1,2,0:T(2,128)(2,1)} %copy.25), calls=%async_computation.1 | async-start | bytes 4194304 | tf_op jit(solution)/shard_map/all_to_all | solution.py:63
  41.9 193.5 %all-gather.3.cloned.1.call-start = ((), (), s32[]{:S(2)}) async-start(), calls=%async_computation.4 | async-start | bytes 3686400 | tf_op jit(solution)/shard_map/all_gather | solution.py:129
  42.7 282.1 %all-reduce.3.cloned.1.call-start = ((), (), s32[]{:S(2)}) async-start(), calls=%async_computation.6 | async-start | bytes 5242880 | tf_op jit(solution)/shard_map/psum | solution.py:144
  130.1 93.4 %copy-start.2 = (f32[1280]{0:T(1024)S(1)}, f32[1280]{0:T(1024)}, u32[]{:S(2)}) copy-start(f32[1280]{0:T(1024)} %param.25) | copy-start | bytes 15364
  225.7 3.7 copy-start.3
  225.7 3.7 copy-start.6
  225.7 3.7 copy-start.7
  235.5 5.9 %copy-start.5 = (bf16[1280,1280]{1,0:T(8,128)(2,1)S(1)}, bf16[1280,1280]{1,0:T(8,128)(2,1)}, u32[]{:S(2)}) copy-start(bf16[1280,1280]{1,0:T(8,128)(2,1)} %all-gather.5.cloned.1.call-done) | copy-start | bytes 9830404
  244.9 154.5 %reduce-scatter.3.cloned.1.call-start = ((), (), s32[]{:S(2)}) async-start(), calls=%async_computation.7 | async-start | bytes 7372800 | tf_op jit(solution)/shard_map/reduce_scatter | solution.py:150
  251.3 221.0 %reduce-scatter.5.cloned.1.call-start = ((), (), s32[]{:S(2)}) async-start(), calls=%async_computation.8 | async-start | bytes 7372800 | tf_op jit(solution)/shard_map/reduce_scatter | solution.py:162
Sparse Core Ops, SparseCore 0:
  9.6 45.8 all-gather.4
  57.2 65.7 all-gather.2
  245.0 79.7 all-reduce.2
  327.0 72.2 reduce-scatter.2
  401.6 70.6 reduce-scatter.4
where the time goes:
time: 482 us; the launch traced here: 481 us
  waiting for transfers between devices  279 us (58%)
  blocking collectives  93.4 us (19%)
  matrix products  43.2 us (9%)
  other arithmetic  20 us (4%)
  local copies, waits for them, and re-layouts  19 us (4%)
  between operations  13.9 us (3%)
  starting transfers between devices  12.4 us (3%)
    psum x1, blocking collectives, project_sum(): return lax.psum(project_terms(clip_blocks, projection), 'llm')  93.4 us
    all_to_all x1, waiting for transfers between devices, deliver(): lax.all_to_all(packed, 'enc', split_axis=0, concat_axis=0, tiled=True)  72.3 us
    reduce_scatter x1, waiting for transfers between devices, shards(): lax.psum_scatter(row_contract(own_columns(post_rounded, jnp.int32(0), dow...  70.9 us
    reduce_scatter x1, waiting for transfers between devices, shards(): lax.psum_scatter(row_contract(own_columns(normed, jnp.int32(0), up_weight...  68.7 us
    psum x1, waiting for transfers between devices, shards(): normed_grad = lax.psum(normed_part, 'llm')  65.7 us
    dot_general x2, matrix products, row_contract(): lax.dot_general(left_rows, right_rows, (((0,), (0,)), ((), ())), preferre...  13.8 us
  transfers between devices with their start and end apart: 7, of which 4 were waited for; matrix products, arithmetic and copies ran while one was open for 15% of the time, Pallas kernels for 0%

commit v1 on v0

--- a/solution.py
+++ b/solution.py
@@ -1,6 +1,8 @@
 import jax
 import jax.numpy as jnp
 from jax import lax
+from jax.experimental import pallas as pl
+from jax.experimental.pallas import tpu as pltpu
 from jax.sharding import PartitionSpec as P
 
 CPS = 2
@@ -175,9 +177,428 @@
     return (input_gradient, up_gradient, down_gradient)
 
 
+MESH = pl.DeviceIdType.MESH
+BF = jnp.bfloat16
+F32 = jnp.float32
+
+W_Z = 0
+W_S = 6
+MARK = 14
+RS1 = 21
+EXCH = 24
+AG = 31
+GS = 34
+GZ = 42
+RS2 = 48
+FIN = 51
+COPIES = 54
+
+
+def dot(left, right, left_dim, right_dim):
+    return lax.dot_general(
+        left, right, (((left_dim,), (right_dim,)), ((), ())), preferred_element_type=F32
+    )
+
+
+def fused_kernel(
+    clips_ref,
+    proj_ref,
+    marks_ref,
+    block_in_ref,
+    block_out_ref,
+    gain_ref,
+    bias_ref,
+    post_gain_ref,
+    up_bias_ref,
+    up_ref,
+    down_ref,
+    input_out,
+    up_out,
+    down_out,
+    weights,
+    marks_in,
+    rs1_send,
+    rs1_recv,
+    exch_send,
+    exch_recv,
+    feat,
+    normed,
+    normed_t,
+    post,
+    post_t,
+    act,
+    slope,
+    pre_grad,
+    rs2_send,
+    rs2_recv,
+    grad_own,
+    gs_send,
+    gs_recv,
+    gz_send,
+    gz_recv,
+    fin_send,
+    send_sems,
+    recv_sems,
+):
+    l = lax.axis_index("llm")
+    e = lax.axis_index("enc")
+    z = e // 2
+    c = e % 2
+    other = z * 2 + 1 - c
+    width = up_ref.shape[1]
+    depth = proj_ref.shape[0]
+    part = up_ref.shape[0]
+    rows = clips_ref.shape[0]
+    own = rows // 4
+    tile = 256
+    chunk = 64
+    scale = 1.0 / (8 * 16)
+
+    def copy(src, dst, index, device):
+        return pltpu.make_async_remote_copy(
+            src_ref=src,
+            dst_ref=dst,
+            send_sem=send_sems.at[index],
+            recv_sem=recv_sems.at[index],
+            device_id=device,
+            device_id_type=MESH,
+        )
+
+    barrier = pltpu.get_barrier_semaphore()
+    for k in range(1, 4):
+        pl.semaphore_signal(barrier, inc=1, device_id=((l + k) % 4, e), device_id_type=MESH)
+    for k in range(1, 8):
+        pl.semaphore_signal(barrier, inc=1, device_id=(l, (e + k) % 8), device_id_type=MESH)
+    pl.semaphore_wait(barrier, 10)
+
+    sent = []
+
+    def start(*args):
+        one = copy(*args)
+        one.start()
+        sent.append(one)
+        return one
+
+    mark_copies = [
+        start(marks_ref.at[(e + k) % 8], marks_in.at[e], MARK + k - 1, (l, (e + k) % 8))
+        for k in range(1, 8)
+    ]
+    marks_in[e] = marks_ref[e]
+    z_copies = []
+    own_copies = []
+    for kind, ref in enumerate((up_ref, down_ref)):
+        z_copies.append(
+            [
+                start(
+                    ref,
+                    weights.at[kind, e],
+                    W_Z + 3 * kind + k - 1,
+                    (l, ((z + k) % 4) * 2 + c),
+                )
+                for k in range(1, 4)
+            ]
+        )
+        own_copies.append(start(ref, weights.at[kind, e], W_S + 4 * kind, (l, other)))
+        weights[kind, e] = ref[...]
+
+    @pl.loop(0, depth // tile)
+    def _(t):
+        columns = pl.ds(pl.multiple_of(t * tile, tile), tile)
+        rs1_send[:, columns] = dot(clips_ref[...], proj_ref[columns, :], 1, 1).astype(BF)
+
+    def rows_of(index):
+        return pl.ds(pl.multiple_of(index * own, own), own)
+
+    rs1_copies = [
+        start(rs1_send.at[rows_of((l + k) % 4), :], rs1_recv.at[k - 1], RS1 + k - 1, ((l + k) % 4, e))
+        for k in range(1, 4)
+    ]
+
+    @pl.loop(0, rows // chunk)
+    def _(t):
+        at = pl.ds(pl.multiple_of(t * chunk, chunk), chunk)
+        hat, _ = norm_stats(block_in_ref[at, :].astype(F32))
+        normed[at, :] = (hat * gain_ref[...] + bias_ref[...]).astype(BF)
+
+    @pl.loop(0, depth // 128)
+    def _(t):
+        at = pl.ds(pl.multiple_of(t * 128, 128), 128)
+        normed_t[at, :] = normed[:, at].T
+
+    for one in rs1_copies:
+        one.wait_recv()
+    total = rs1_send[rows_of(l), :].astype(F32)
+    for k in range(3):
+        total += rs1_recv[k].astype(F32)
+    exch_send[...] = total.astype(BF).reshape(exch_send.shape)
+    exch_copies = [
+        start(exch_send.at[(e + k) % 8], exch_recv.at[e], EXCH + k - 1, (l, (e + k) % 8))
+        for k in range(1, 8)
+    ]
+    exch_recv[e] = exch_send[e]
+    for one in mark_copies:
+        one.wait_recv()
+    for one in exch_copies:
+        one.wait_recv()
+    feat[rows_of(l), :] = dot(
+        marks_in[...].reshape(own, own), exch_recv[...].reshape(own, depth), 0, 0
+    ).astype(BF)
+    ag_copies = [
+        start(feat.at[rows_of(l), :], feat.at[rows_of(l), :], AG + k - 1, ((l + k) % 4, e))
+        for k in range(1, 4)
+    ]
+
+    def gather_weight(kind):
+        passed = [own_copies[kind]]
+        for k in range(1, 4):
+            z_copies[kind][k - 1].wait_recv()
+            block = weights.at[kind, ((z - k + 4) % 4) * 2 + c]
+            passed.append(start(block, block, W_S + 4 * kind + k, (l, other)))
+        for one in passed:
+            one.wait_recv()
+
+    def whole(kind):
+        return weights[kind].reshape(depth, width)
+
+    gather_weight(0)
+
+    @pl.loop(0, width // tile)
+    def _(t):
+        at = pl.ds(pl.multiple_of(t * tile, tile), tile)
+        up_tile = weights[0, :, :, at].reshape(depth, tile)
+        pre_act = dot(normed[...], up_tile, 1, 0) + up_bias_ref[:, at]
+        activation, gelu_slope = gelu_parts(pre_act)
+        act[:, at] = activation.astype(BF)
+        slope[:, at] = gelu_slope
+
+    def post_rows(at):
+        hat, inverse = norm_stats(block_out_ref[at, :].astype(F32))
+        return norm_backward(feat[at, :].astype(F32) * post_gain_ref[...], hat, inverse)
+
+    for one in ag_copies:
+        one.wait_recv()
+
+    @pl.loop(0, rows // chunk)
+    def _(t):
+        at = pl.ds(pl.multiple_of(t * chunk, chunk), chunk)
+        post[at, :] = post_rows(at).astype(BF)
+
+    @pl.loop(0, depth // 128)
+    def _(t):
+        at = pl.ds(pl.multiple_of(t * 128, 128), 128)
+        post_t[at, :] = post[:, at].T
+
+    def weight_terms(kind, left_t, right):
+        def term(block):
+            left = left_t[pl.ds(pl.multiple_of(block * part, part), part), :]
+            return dot(left, right[...], 1, 0)
+
+        copies = []
+        for k in range(4):
+            zk = (z + k) % 4
+            gs_send[kind, k] = term(zk * 2 + 1 - c).astype(BF)
+            copies.append(
+                start(gs_send.at[kind, k], gs_recv.at[kind, k], GS + 4 * kind + k, (l, other))
+            )
+        for k in range(4):
+            zk = (z + k) % 4
+            grad_own[kind, k] = term(zk * 2 + c)
+        return copies
+
+    def weight_sums(kind, copies):
+        sums = []
+        for k in (1, 2, 3):
+            copies[k].wait_recv()
+            both = grad_own[kind, k] + gs_recv[kind, k].astype(F32)
+            gz_send[kind, k - 1] = both.astype(BF)
+            sums.append(
+                start(
+                    gz_send.at[kind, k - 1],
+                    gz_recv.at[kind, k - 1],
+                    GZ + 3 * kind + k - 1,
+                    (l, ((z + k) % 4) * 2 + c),
+                )
+            )
+        copies[0].wait_recv()
+        return sums
+
+    def weight_result(kind, sums, out):
+        for one in sums:
+            one.wait_recv()
+        total = grad_own[kind, 0] + gs_recv[kind, 0].astype(F32)
+        for k in range(3):
+            total += gz_recv[kind, k].astype(F32)
+        out[...] = total * scale
+
+    down_copies = weight_terms(1, post_t, act)
+    down_sums = weight_sums(1, down_copies)
+
+    gather_weight(1)
+
+    @pl.loop(0, width // tile)
+    def _(t):
+        at = pl.ds(pl.multiple_of(t * tile, tile), tile)
+        down_tile = weights[1, :, :, at].reshape(depth, tile)
+        pre_grad[:, at] = (dot(post[...], down_tile, 1, 0) * slope[:, at]).astype(BF)
+
+    up_copies = weight_terms(0, normed_t, pre_grad)
+    up_sums = weight_sums(0, up_copies)
+
+    for k in range(8):
+        rs2_send[:, k * part : (k + 1) * part] = dot(pre_grad[...], weights[0, k], 1, 1).astype(BF)
+    rs2_copies = [
+        start(rs2_send.at[rows_of((l + k) % 4), :], rs2_recv.at[k - 1], RS2 + k - 1, ((l + k) % 4, e))
+        for k in range(1, 4)
+    ]
+    for one in rs2_copies:
+        one.wait_recv()
+    normed_grad = rs2_send[rows_of(l), :].astype(F32)
+    for k in range(3):
+        normed_grad += rs2_recv[k].astype(F32)
+    hat, inverse = norm_stats(block_in_ref[rows_of(l), :].astype(F32))
+    result = post_rows(rows_of(l)) + norm_backward(normed_grad * gain_ref[...], hat, inverse)
+    share = depth // 4
+    for j in range(4):
+        fin_send[j] = result[:, j * share : (j + 1) * share].astype(BF)
+    fin_copies = [
+        start(fin_send.at[(l + k) % 4], input_out.at[l], FIN + k - 1, ((l + k) % 4, e))
+        for k in range(1, 4)
+    ]
+    input_out[l] = fin_send[l]
+
+    weight_result(1, down_sums, down_out)
+    weight_result(0, up_sums, up_out)
+    for one in fin_copies:
+        one.wait_recv()
+    for one in sent:
+        one.wait_send()
+
+
+def fused_shards(
+    token_gradient,
+    projection,
+    clip_length,
+    clip_offset,
+    clip_home,
+    block_input,
+    block_output,
+    norm_gain,
+    norm_bias,
+    up_weight,
+    up_bias,
+    down_weight,
+    post_gain,
+):
+    groups = lax.axis_size("llm")
+    devices = lax.axis_size("enc")
+    clips_here, frames, depth = block_input.shape
+    sequences, sequence_rows, columns = token_gradient.shape
+    pair_slots = clips_here // devices
+    rows = clips_here * frames
+    piece = frames // groups
+    own = rows // groups
+    clip_order = jnp.arange(clips_here, dtype=jnp.int32)
+    target = clip_home // clips_here
+    slot_place = clip_home % clips_here
+    earlier = clip_order[None, :] < clip_order[:, None]
+    same_target = target[None, :] == target[:, None]
+    bucket_rank = jnp.sum((earlier & same_target).astype(jnp.int32), axis=1)
+    bucket = target * pair_slots + bucket_rank
+    in_bucket = (clip_order[:, None] == bucket[None, :]).astype(jnp.int32)
+
+    def by_bucket(values):
+        return jnp.sum(in_bucket * values[None, :], axis=1)
+
+    first_row = by_bucket((clip_order // CPS) * sequence_rows + clip_offset)
+    lengths = by_bucket(clip_length)
+    places = by_bucket(slot_place)
+    frame = jnp.arange(frames, dtype=jnp.int32).reshape(groups, 1, piece)
+    source = jnp.where(
+        frame < lengths[None, :, None], first_row[None, :, None] + frame, -1
+    ).reshape(rows)
+    token_rows = jnp.arange(sequences * sequence_rows, dtype=jnp.int32)
+    picks = (source[:, None] == token_rows[None, :]).astype(BF)
+    clips = jnp.dot(
+        picks,
+        token_gradient.reshape(sequences * sequence_rows, columns),
+        preferred_element_type=F32,
+    ).astype(BF)
+    goal = (places[:, None] * piece + jnp.arange(piece, dtype=jnp.int32)[None, :]).reshape(own)
+    marks = (goal[:, None] == jnp.arange(own, dtype=jnp.int32)[None, :]).astype(BF)
+    marks = marks.reshape(devices, pair_slots * piece, own)
+
+    def by_part(values):
+        return (
+            values.reshape(clips_here, groups, piece, depth).swapaxes(0, 1).reshape(rows, depth)
+        )
+
+    part, width = up_weight.shape
+    share = depth // groups
+    vmem = pl.BlockSpec(memory_space=pltpu.VMEM)
+    exchange = (devices, own // devices, depth)
+    input_parts, up_gradient, down_gradient = pl.pallas_call(
+        fused_kernel,
+        out_shape=(
+            jax.ShapeDtypeStruct((groups, own, share), BF),
+            jax.ShapeDtypeStruct((part, width), F32),
+            jax.ShapeDtypeStruct((part, width), F32),
+        ),
+        in_specs=[vmem] * 11,
+        out_specs=(vmem, vmem, vmem),
+        scratch_shapes=[
+            pltpu.VMEM((2, devices, part, width), BF),
+            pltpu.VMEM(marks.shape, BF),
+            pltpu.VMEM((rows, depth), BF),
+            pltpu.VMEM((3, own, depth), BF),
+            pltpu.VMEM(exchange, BF),
+            pltpu.VMEM(exchange, BF),
+            pltpu.VMEM((rows, depth), BF),
+            pltpu.VMEM((rows, depth), BF),
+            pltpu.VMEM((depth, rows), BF),
+            pltpu.VMEM((rows, depth), BF),
+            pltpu.VMEM((depth, rows), BF),
+            pltpu.VMEM((rows, width), BF),
+            pltpu.VMEM((rows, width), F32),
+            pltpu.VMEM((rows, width), BF),
+            pltpu.VMEM((rows, depth), BF),
+            pltpu.VMEM((3, own, depth), BF),
+            pltpu.VMEM((2, 4, part, width), F32),
+            pltpu.VMEM((2, 4, part, width), BF),
+            pltpu.VMEM((2, 4, part, width), BF),
+            pltpu.VMEM((2, 3, part, width), BF),
+            pltpu.VMEM((2, 3, part, width), BF),
+            pltpu.VMEM((groups, own, share), BF),
+            pltpu.SemaphoreType.DMA((COPIES,)),
+            pltpu.SemaphoreType.DMA((COPIES,)),
+        ],
+        compiler_params=pltpu.CompilerParams(
+            collective_id=0, has_side_effects=True, vmem_limit_bytes=62 * 1024 * 1024
+        ),
+    )(
+        clips,
+        projection,
+        marks,
+        by_part(block_input),
+        by_part(block_output),
+        norm_gain.reshape(1, depth),
+        norm_bias.reshape(1, depth),
+        post_gain.reshape(1, depth),
+        up_bias.reshape(1, width),
+        up_weight,
+        down_weight.T,
+    )
+    input_gradient = (
+        input_parts.reshape(groups, clips_here, piece, share)
+        .swapaxes(0, 1)
+        .reshape(clips_here, frames, share)
+    )
+    return (input_gradient, up_gradient, down_gradient.T)
+
+
 def solution(mesh):
+    fused = mesh.shape["llm"] == 4 and mesh.shape["enc"] == 8
     return jax.shard_map(
-        shards,
+        fused_shards if fused else shards,
         mesh=mesh,
         in_specs=(
             P("enc", None, "llm"),

time: 482 us -> 207 us (0.43)
  the two profiles are of different devices: /device:TPU:0 before, /device:TPU:8 now
where the time goes in v1:
time: 207 us
  Pallas kernels  184 us (89%)
  local copies, waits for them, and re-layouts  14 us (7%)
  matrix products  5.92 us (3%)
  other arithmetic  2.57 us (1%)
    pallas_call x1, Pallas kernels, fused_shards(): pl.pallas_call(fused_kernel, out_shape=(jax.ShapeDtypeStruct((groups, own...  184 us
    dot_general x1, matrix products, fused_shards(): jnp.dot(picks, token_gradient.reshape(sequences * sequence_rows, columns)...  5.92 us

profile of v1, /device:TPU:8, one launch (start us, length us, event | category | flops | bytes accessed | tf_op | source)
XLA Modules:
  0.0 206.8 jit_solution(12182430217426870754)
XLA Ops:
  0.6 0.0 copy-start
  0.6 0.8 and_select_fusion.2
  1.4 0.2 convert_reduce_fusion
  1.6 0.8 select_reduce_fusion
  2.4 0.1 mul.51
  2.5 0.1 add.65
  2.6 0.1 add.66
  2.7 1.3 reshape.141.gain_ref
  4.0 1.3 reshape.142.bias_ref
  5.3 1.3 reshape.144.up_bias_ref
  6.6 1.3 reshape.143.post_gain_ref
  7.9 0.1 add.68
  7.9 0.7 fusion.1.marks_ref
  8.6 0.1 add_select_fusion
  8.7 0.1 select_n.29
  8.8 2.5 %copy.22 = bf16[16,4,8,1280]{3,2,0,1:T(8,128)(2,1)} copy(bf16[16,4,8,1280]{3,2,1,0:T(8,128)(2,1)} %bitcast.21) | data formatting | bytes 2621440 | tf_op jit(solution)/shard_map/reshape | solution.py:532
  11.3 0.0 copy-done
  11.3 1.1 copy.23
  12.4 5.9 %convolution_convert_fusion.clips_ref = bf16[512,2048]{1,0:T(8,128)(2,1)} fusion(bf16[1024,2048]{1,0:T(8,128)(2,1)} %bitcast.25, s32[512]{0:T(512)S(1)} %select_n.29), kind=kOutput, calls=%fused_computation | convolution fusion | flops 2149056512 | bytes 6293504 | tf_op jit(solution)/shard_map/dot_general | solution.py:521
  18.3 183.6 %shard_map.148 = (bf16[4,128,320]{2,1,0:T(8,128)(2,1)}, f32[160,1280]{1,0:T(8,128)}, f32[160,1280]{1,0:T(8,128)}) custom-call(bf16[512,2048]{1,0:T(8,128)(2,1)} %convolution_convert_fusion.clips_ref, bf16[1280,2048]{1,0:T(8,128)(2,1)} %proj_ref.1, bf16[8,16,128]{2,1,0:T(8,128)(2,1)} %fusion.1.marks_ref, bf16[512,1280]{1,0:T(8,128)(2,1)} %bitcast.19, ...), custom_call_target="tpu_custom_call" | custom-call | tf_op jit(solution)/shard_map/pallas_call | solution.py:539
  201.9 0.0 copy-start.1
  201.9 1.9 copy_bitcast_fusion
  203.8 2.1 %copy.28 = f32[160,1280]{1,0:T(8,128)} copy(f32[160,1280]{1,0:T(8,128)} %get-tuple-element.19) | data formatting | bytes 1638400
  205.9 0.9 copy.29
  (6 shorter events, 0.0 us)
Async XLA Ops:
  0.6 10.6 %copy-start = (bf16[16,32,1280]{2,1,0:T(8,128)(2,1)S(1)}, bf16[16,32,1280]{2,1,0:T(8,128)(2,1)}, u32[]{:S(2)}) copy-start(bf16[16,32,1280]{2,1,0:T(8,128)(2,1)} %param.19) | copy-start | bytes 3932164
  201.9 4.0 %copy-start.1 = (f32[160,1280]{1,0:T(8,128)S(1)}, f32[160,1280]{1,0:T(8,128)}, u32[]{:S(2)}) copy-start(f32[160,1280]{1,0:T(8,128)} %get-tuple-element.8) | copy-start | bytes 2457604

commit v2 on v1

--- a/solution.py
+++ b/solution.py
@@ -181,17 +181,19 @@
 BF = jnp.bfloat16
 F32 = jnp.float32
 
-W_Z = 0
-W_S = 6
-MARK = 14
-RS1 = 21
-EXCH = 24
-AG = 31
-GS = 34
-GZ = 42
-RS2 = 48
-FIN = 51
-COPIES = 54
+W_RIGHT = 0
+W_LEFT = 8
+W_S = 16
+MARK = 24
+RS1 = 31
+EXCH = 34
+AG = 41
+GS = 44
+C_RIGHT = 52
+C_LEFT = 60
+RS2 = 68
+FIN = 71
+COPIES = 74
 
 
 def dot(left, right, left_dim, right_dim):
@@ -201,20 +203,21 @@
 
 
 def fused_kernel(
-    clips_ref,
-    proj_ref,
+    tokens_hbm,
+    source_ref,
+    proj_hbm,
     marks_ref,
     block_in_ref,
     block_out_ref,
-    gain_ref,
-    bias_ref,
-    post_gain_ref,
-    up_bias_ref,
+    vectors_ref,
     up_ref,
     down_ref,
     input_out,
     up_out,
     down_out,
+    tokens_ref,
+    proj_ref,
+    clips_ref,
     weights,
     marks_in,
     rs1_send,
@@ -229,14 +232,14 @@
     act,
     slope,
     pre_grad,
-    rs2_send,
     rs2_recv,
     grad_own,
     gs_send,
     gs_recv,
-    gz_send,
-    gz_recv,
+    chain_send,
+    chain_recv,
     fin_send,
+    load_sems,
     send_sems,
     recv_sems,
 ):
@@ -264,6 +267,16 @@
             device_id_type=MESH,
         )
 
+    loads = [
+        pltpu.make_async_copy(tokens_hbm, tokens_ref, load_sems.at[0]),
+        pltpu.make_async_copy(proj_hbm, proj_ref, load_sems.at[1]),
+    ]
+    for one in loads:
+        one.start()
+    gain = vectors_ref[0:1, :]
+    bias = vectors_ref[1:2, :]
+    post_gain = vectors_ref[2:3, :]
+
     barrier = pltpu.get_barrier_semaphore()
     for k in range(1, 4):
         pl.semaphore_signal(barrier, inc=1, device_id=((l + k) % 4, e), device_id_type=MESH)
@@ -279,27 +292,92 @@
         sent.append(one)
         return one
 
+    def device_at(z_to):
+        return (l, z_to * 2 + c)
+
+    def pass_block(kind, block_z, step, action):
+        block = weights.at[kind, block_z * 2 + c]
+
+        def over(index, device):
+            return copy(block, block, index + 4 * kind + block_z, device)
+
+        across = over(W_S, (l, other))
+
+        def along(index, z_to):
+            if action == "send":
+                over(index, device_at(z_to)).start()
+            else:
+                over(index, device_at(z_to)).wait_send()
+
+        if action == "send":
+            across.start()
+        else:
+            across.wait_send()
+        return along, over
+
+    def hop(kind, step, action="send"):
+        if step == 0:
+            along, _ = pass_block(kind, z, 0, action)
+
+            @pl.when(z < 3)
+            def _():
+                along(W_RIGHT, z + 1)
+
+            @pl.when(z > 0)
+            def _():
+                along(W_LEFT, z - 1)
+
+            return
+
+        @pl.when(z >= step)
+        def _():
+            block_z = z - step
+            if action == "send":
+                block = weights.at[kind, block_z * 2 + c]
+                copy(block, block, W_RIGHT + 4 * kind + block_z, device_at(z - 1)).wait_recv()
+            along, _ = pass_block(kind, block_z, step, action)
+
+            @pl.when(z < 3)
+            def _():
+                along(W_RIGHT, z + 1)
+
+        @pl.when(z + step <= 3)
+        def _():
+            block_z = z + step
+            if action == "send":
+                block = weights.at[kind, block_z * 2 + c]
+                copy(block, block, W_LEFT + 4 * kind + block_z, device_at(z + 1)).wait_recv()
+            along, _ = pass_block(kind, block_z, step, action)
+
+            @pl.when(z > 0)
+            def _():
+                along(W_LEFT, z - 1)
+
+    def whole_weight(kind):
+        for block_z in range(4):
+            block = weights.at[kind, block_z * 2 + 1 - c]
+            copy(block, block, W_S + 4 * kind + block_z, (l, other)).wait_recv()
+
+    weights[0, e] = up_ref[...]
+    hop(0, 0)
     mark_copies = [
         start(marks_ref.at[(e + k) % 8], marks_in.at[e], MARK + k - 1, (l, (e + k) % 8))
         for k in range(1, 8)
     ]
     marks_in[e] = marks_ref[e]
-    z_copies = []
-    own_copies = []
-    for kind, ref in enumerate((up_ref, down_ref)):
-        z_copies.append(
-            [
-                start(
-                    ref,
-                    weights.at[kind, e],
-                    W_Z + 3 * kind + k - 1,
-                    (l, ((z + k) % 4) * 2 + c),
-                )
-                for k in range(1, 4)
-            ]
-        )
-        own_copies.append(start(ref, weights.at[kind, e], W_S + 4 * kind, (l, other)))
-        weights[kind, e] = ref[...]
+    weights[1, e] = down_ref[...]
+
+    token_rows = tokens_ref.shape[0]
+    order = lax.broadcasted_iota(jnp.int32, (rows, token_rows), 1)
+    act[:, :token_rows] = jnp.where(source_ref[...] == order, 1.0, 0.0).astype(BF)
+    loads[0].wait()
+
+    @pl.loop(0, clips_ref.shape[1] // tile)
+    def _(t):
+        columns = pl.ds(pl.multiple_of(t * tile, tile), tile)
+        clips_ref[:, columns] = dot(act[:, :token_rows], tokens_ref[:, columns], 1, 0).astype(BF)
+
+    loads[1].wait()
 
     @pl.loop(0, depth // tile)
     def _(t):
@@ -318,13 +396,15 @@
     def _(t):
         at = pl.ds(pl.multiple_of(t * chunk, chunk), chunk)
         hat, _ = norm_stats(block_in_ref[at, :].astype(F32))
-        normed[at, :] = (hat * gain_ref[...] + bias_ref[...]).astype(BF)
+        normed[at, :] = (hat * gain + bias).astype(BF)
 
     @pl.loop(0, depth // 128)
     def _(t):
         at = pl.ds(pl.multiple_of(t * 128, 128), 128)
         normed_t[at, :] = normed[:, at].T
 
+    hop(0, 1)
+    hop(1, 0)
     for one in rs1_copies:
         one.wait_recv()
     total = rs1_send[rows_of(l), :].astype(F32)
@@ -336,6 +416,7 @@
         for k in range(1, 8)
     ]
     exch_recv[e] = exch_send[e]
+    hop(0, 2)
     for one in mark_copies:
         one.wait_recv()
     for one in exch_copies:
@@ -348,33 +429,24 @@
         for k in range(1, 4)
     ]
 
-    def gather_weight(kind):
-        passed = [own_copies[kind]]
-        for k in range(1, 4):
-            z_copies[kind][k - 1].wait_recv()
-            block = weights.at[kind, ((z - k + 4) % 4) * 2 + c]
-            passed.append(start(block, block, W_S + 4 * kind + k, (l, other)))
-        for one in passed:
-            one.wait_recv()
-
-    def whole(kind):
-        return weights[kind].reshape(depth, width)
-
-    gather_weight(0)
+    hop(1, 1)
+    hop(0, 3)
+    whole_weight(0)
 
     @pl.loop(0, width // tile)
     def _(t):
         at = pl.ds(pl.multiple_of(t * tile, tile), tile)
         up_tile = weights[0, :, :, at].reshape(depth, tile)
-        pre_act = dot(normed[...], up_tile, 1, 0) + up_bias_ref[:, at]
+        pre_act = dot(normed[...], up_tile, 1, 0) + vectors_ref[3:4, at]
         activation, gelu_slope = gelu_parts(pre_act)
         act[:, at] = activation.astype(BF)
         slope[:, at] = gelu_slope
 
     def post_rows(at):
         hat, inverse = norm_stats(block_out_ref[at, :].astype(F32))
-        return norm_backward(feat[at, :].astype(F32) * post_gain_ref[...], hat, inverse)
-
+        return norm_backward(feat[at, :].astype(F32) * post_gain, hat, inverse)
+
+    hop(1, 2)
     for one in ag_copies:
         one.wait_recv()
 
@@ -395,45 +467,93 @@
 
         copies = []
         for k in range(4):
-            zk = (z + k) % 4
-            gs_send[kind, k] = term(zk * 2 + 1 - c).astype(BF)
+            gs_send[kind, k] = term(k * 2 + 1 - c).astype(BF)
             copies.append(
                 start(gs_send.at[kind, k], gs_recv.at[kind, k], GS + 4 * kind + k, (l, other))
             )
         for k in range(4):
-            zk = (z + k) % 4
-            grad_own[kind, k] = term(zk * 2 + c)
-        return copies
-
-    def weight_sums(kind, copies):
-        sums = []
-        for k in (1, 2, 3):
-            copies[k].wait_recv()
-            both = grad_own[kind, k] + gs_recv[kind, k].astype(F32)
-            gz_send[kind, k - 1] = both.astype(BF)
-            sums.append(
-                start(
-                    gz_send.at[kind, k - 1],
-                    gz_recv.at[kind, k - 1],
-                    GZ + 3 * kind + k - 1,
-                    (l, ((z + k) % 4) * 2 + c),
-                )
-            )
-        copies[0].wait_recv()
-        return sums
-
-    def weight_result(kind, sums, out):
-        for one in sums:
+            grad_own[kind, k] = term(k * 2 + c)
+        for one in copies:
             one.wait_recv()
-        total = grad_own[kind, 0] + gs_recv[kind, 0].astype(F32)
-        for k in range(3):
-            total += gz_recv[kind, k].astype(F32)
-        out[...] = total * scale
-
-    down_copies = weight_terms(1, post_t, act)
-    down_sums = weight_sums(1, down_copies)
-
-    gather_weight(1)
+
+    def chain_copy(kind, to_z, step):
+        slot = jnp.where(to_z == z + step, 4, to_z) if step < 0 else to_z
+        return copy(
+            chain_send.at[kind, to_z],
+            chain_recv.at[kind, slot],
+            (C_RIGHT if step > 0 else C_LEFT) + 4 * kind + to_z,
+            device_at(z + step),
+        )
+
+    def received(kind, to_z, step):
+        slot = jnp.where(to_z == z, 4, to_z) if step < 0 else to_z
+        block = chain_recv.at[kind, slot]
+        index = (C_RIGHT if step > 0 else C_LEFT) + 4 * kind + to_z
+        copy(block, block, index, device_at(z - step)).wait_recv()
+        return chain_recv[kind, slot].astype(F32)
+
+    def chain_ends(kind):
+        def send(to_z, step):
+            total = grad_own[kind, to_z] + gs_recv[kind, to_z].astype(F32)
+            chain_send[kind, to_z] = total.astype(BF)
+            chain_copy(kind, to_z, step).start()
+
+        @pl.when(z == 0)
+        def _():
+            for to_z in (3, 2, 1):
+                send(to_z, 1)
+
+        @pl.when(z == 3)
+        def _():
+            for to_z in (0, 1, 2):
+                send(to_z, -1)
+
+    def chain_middle(kind):
+        def send(to_z, step):
+            total = grad_own[kind, to_z] + gs_recv[kind, to_z].astype(F32)
+            chain_send[kind, to_z] = (total + received(kind, to_z, step)).astype(BF)
+            chain_copy(kind, to_z, step).start()
+
+        @pl.when(z == 1)
+        def _():
+            send(3, 1)
+            send(2, 1)
+            send(0, -1)
+
+        @pl.when(z == 2)
+        def _():
+            send(0, -1)
+            send(1, -1)
+            send(3, 1)
+
+    def weight_result(kind, out):
+        out[...] = grad_own[kind, z] + gs_recv[kind, z].astype(F32)
+
+        @pl.when(z > 0)
+        def _():
+            out[...] += received(kind, z, 1)
+
+        @pl.when(z < 3)
+        def _():
+            out[...] += received(kind, z, -1)
+
+        out[...] *= scale
+
+    def chain_done(kind):
+        for to_z in range(4):
+
+            @pl.when(z < to_z)
+            def _():
+                chain_copy(kind, to_z, 1).wait_send()
+
+            @pl.when(z > to_z)
+            def _():
+                chain_copy(kind, to_z, -1).wait_send()
+
+    weight_terms(1, post_t, act)
+    chain_ends(1)
+    hop(1, 3)
+    whole_weight(1)
 
     @pl.loop(0, width // tile)
     def _(t):
@@ -441,22 +561,26 @@
         down_tile = weights[1, :, :, at].reshape(depth, tile)
         pre_grad[:, at] = (dot(post[...], down_tile, 1, 0) * slope[:, at]).astype(BF)
 
-    up_copies = weight_terms(0, normed_t, pre_grad)
-    up_sums = weight_sums(0, up_copies)
-
+    weight_terms(0, normed_t, pre_grad)
+    chain_ends(0)
+    for one in rs1_copies:
+        one.wait_send()
+    sent[:] = [one for one in sent if not any(one is early for early in rs1_copies)]
+    rs2_send = rs1_send
     for k in range(8):
         rs2_send[:, k * part : (k + 1) * part] = dot(pre_grad[...], weights[0, k], 1, 1).astype(BF)
     rs2_copies = [
         start(rs2_send.at[rows_of((l + k) % 4), :], rs2_recv.at[k - 1], RS2 + k - 1, ((l + k) % 4, e))
         for k in range(1, 4)
     ]
+    chain_middle(1)
     for one in rs2_copies:
         one.wait_recv()
     normed_grad = rs2_send[rows_of(l), :].astype(F32)
     for k in range(3):
         normed_grad += rs2_recv[k].astype(F32)
     hat, inverse = norm_stats(block_in_ref[rows_of(l), :].astype(F32))
-    result = post_rows(rows_of(l)) + norm_backward(normed_grad * gain_ref[...], hat, inverse)
+    result = post_rows(rows_of(l)) + norm_backward(normed_grad * gain, hat, inverse)
     share = depth // 4
     for j in range(4):
         fin_send[j] = result[:, j * share : (j + 1) * share].astype(BF)
@@ -466,12 +590,17 @@
     ]
     input_out[l] = fin_send[l]
 
-    weight_result(1, down_sums, down_out)
-    weight_result(0, up_sums, up_out)
+    chain_middle(0)
+    weight_result(1, down_out)
+    weight_result(0, up_out)
     for one in fin_copies:
         one.wait_recv()
     for one in sent:
         one.wait_send()
+    for kind in range(2):
+        for step in range(4):
+            hop(kind, step, "wait")
+        chain_done(kind)
 
 
 def fused_shards(
@@ -516,13 +645,6 @@
     source = jnp.where(
         frame < lengths[None, :, None], first_row[None, :, None] + frame, -1
     ).reshape(rows)
-    token_rows = jnp.arange(sequences * sequence_rows, dtype=jnp.int32)
-    picks = (source[:, None] == token_rows[None, :]).astype(BF)
-    clips = jnp.dot(
-        picks,
-        token_gradient.reshape(sequences * sequence_rows, columns),
-        preferred_element_type=F32,
-    ).astype(BF)
     goal = (places[:, None] * piece + jnp.arange(piece, dtype=jnp.int32)[None, :]).reshape(own)
     marks = (goal[:, None] == jnp.arange(own, dtype=jnp.int32)[None, :]).astype(BF)
     marks = marks.reshape(devices, pair_slots * piece, own)
@@ -535,6 +657,7 @@
     part, width = up_weight.shape
     share = depth // groups
     vmem = pl.BlockSpec(memory_space=pltpu.VMEM)
+    anywhere = pl.BlockSpec(memory_space=pl.ANY)
     exchange = (devices, own // devices, depth)
     input_parts, up_gradient, down_gradient = pl.pallas_call(
         fused_kernel,
@@ -543,9 +666,12 @@
             jax.ShapeDtypeStruct((part, width), F32),
             jax.ShapeDtypeStruct((part, width), F32),
         ),
-        in_specs=[vmem] * 11,
+        in_specs=[anywhere, vmem, anywhere] + [vmem] * 6,
         out_specs=(vmem, vmem, vmem),
         scratch_shapes=[
+            pltpu.VMEM((sequences * sequence_rows, columns), BF),
+            pltpu.VMEM((depth, columns), BF),
+            pltpu.VMEM((rows, columns), BF),
             pltpu.VMEM((2, devices, part, width), BF),
             pltpu.VMEM(marks.shape, BF),
             pltpu.VMEM((rows, depth), BF),
@@ -560,14 +686,14 @@
             pltpu.VMEM((rows, width), BF),
             pltpu.VMEM((rows, width), F32),
             pltpu.VMEM((rows, width), BF),
-            pltpu.VMEM((rows, depth), BF),
             pltpu.VMEM((3, own, depth), BF),
             pltpu.VMEM((2, 4, part, width), F32),
             pltpu.VMEM((2, 4, part, width), BF),
             pltpu.VMEM((2, 4, part, width), BF),
-            pltpu.VMEM((2, 3, part, width), BF),
-            pltpu.VMEM((2, 3, part, width), BF),
+            pltpu.VMEM((2, 4, part, width), BF),
+            pltpu.VMEM((2, 5, part, width), BF),
             pltpu.VMEM((groups, own, share), BF),
+            pltpu.SemaphoreType.DMA((2,)),
             pltpu.SemaphoreType.DMA((COPIES,)),
             pltpu.SemaphoreType.DMA((COPIES,)),
         ],
@@ -575,15 +701,13 @@
             collective_id=0, has_side_effects=True, vmem_limit_bytes=62 * 1024 * 1024
         ),
     )(
-        clips,
+        token_gradient.reshape(sequences * sequence_rows, columns),
+        source.reshape(rows, 1),
         projection,
         marks,
         by_part(block_input),
         by_part(block_output),
-        norm_gain.reshape(1, depth),
-        norm_bias.reshape(1, depth),
-        post_gain.reshape(1, depth),
-        up_bias.reshape(1, width),
+        jnp.stack([norm_gain, norm_bias, post_gain, up_bias]),
         up_weight,
         down_weight.T,
     )

time: 207 us -> 146 us (0.71)
  the two profiles are of different devices: /device:TPU:8 before, /device:TPU:0 now
where the time goes in v2:
time: 146 us
  Pallas kernels  130 us (89%)
  local copies, waits for them, and re-layouts  12.5 us (9%)
  other arithmetic  3.09 us (2%)
    pallas_call x1, Pallas kernels, fused_shards(): pl.pallas_call(fused_kernel, out_shape=(jax.ShapeDtypeStruct((groups, own...  130 us
    reshape x2, local copies, waits for them, and re-layouts, by_part(): values.reshape(clips_here, groups, piece, depth).swapaxes(0, 1)  3.73 us
    unnamed x6, local copies, waits for them, and re-layouts  2.99 us

profile of v2, /device:TPU:0, one launch (start us, length us, event | category | flops | bytes accessed | tf_op | source)
XLA Modules:
  0.0 145.9 jit_solution(12787210737872626912)
XLA Ops:
  0.6 0.7 and_select_fusion.2
  1.3 0.2 convert_reduce_fusion
  1.5 0.8 select_reduce_fusion
  2.3 0.1 mul.51
  2.4 0.1 add.68
  2.5 0.1 add.69
  2.6 0.7 stack.15
  3.3 0.7 stack.16
  4.0 0.7 stack.18
  4.7 0.7 stack.17
  5.4 0.6 pad_maximum_fusion.vectors_ref
  6.0 0.1 add.71
  6.1 0.7 fusion.marks_ref
  6.8 0.1 add_select_fusion
  6.9 0.8 select_n.34.source_ref
  7.7 2.6 %copy.23 = bf16[16,4,8,1280]{3,2,0,1:T(8,128)(2,1)} copy(bf16[16,4,8,1280]{3,2,1,0:T(8,128)(2,1)} %bitcast.21) | data formatting | bytes 2621440 | tf_op jit(solution)/shard_map/reshape | solution.py:654
  10.3 0.0 copy-done
  10.3 1.2 copy.24
  11.4 129.6 %shard_map.148 = (bf16[4,128,320]{2,1,0:T(8,128)(2,1)}, f32[160,1280]{1,0:T(8,128)}, f32[160,1280]{1,0:T(8,128)}) custom-call(bf16[1024,2048]{1,0:T(8,128)(2,1)} %bitcast.20, s32[512,1]{1,0:T(8,128)} %select_n.34.source_ref, bf16[1280,2048]{1,0:T(8,128)(2,1)} %proj_hbm.1, bf16[8,16,128]{2,1,0:T(8,128)(2,1)} %fusion.marks_ref, bf16[512,1280]{1,0:T(8,128)(2,1)} %bitcast.18, ...), custom_call_target="tpu_custom_call" | custom-call | tf_op jit(solution)/shard_map/pallas_call | solution.py:662
  141.0 0.0 copy-start.1
  141.0 1.9 %copy_bitcast_fusion = bf16[16,32,320]{2,1,0:T(8,128)(2,1)} fusion(bf16[4,128,320]{2,1,0:T(8,128)(2,1)} %get-tuple-element.6), kind=kLoop, calls=%fused_computation | loop fusion | bytes 655360 | tf_op jit(solution)/shard_map/reshape | solution.py:717
  142.9 2.1 %copy.30 = f32[160,1280]{1,0:T(8,128)} copy(f32[160,1280]{1,0:T(8,128)} %get-tuple-element.19) | data formatting | bytes 1638400
  145.0 0.0 copy-done.1
  145.0 0.9 copy.31
  (6 shorter events, 0.0 us)
Async XLA Ops:
  7.7 2.6 %copy-start = (bf16[16,32,1280]{2,1,0:T(8,128)(2,1)S(1)}, bf16[16,32,1280]{2,1,0:T(8,128)(2,1)}, u32[]{:S(2)}) copy-start(bf16[16,32,1280]{2,1,0:T(8,128)(2,1)} %param.19) | copy-start | bytes 3932164
  141.0 4.0 %copy-start.1 = (f32[160,1280]{1,0:T(8,128)S(1)}, f32[160,1280]{1,0:T(8,128)}, u32[]{:S(2)}) copy-start(f32[160,1280]{1,0:T(8,128)} %get-tuple-element.8) | copy-start | bytes 2457604
